TPU v7x, 32 devices: a whole 2x2x4 slice. The times are simulated.
32 devices in a mesh: dp: 2 (over core), expert: 16 (over z, y, x).
Axes of the slice: x: 2, y: 2, z: 4, core: 2. Of those that a mesh axis runs over, the one named last changes fastest.
Arguments:
- tokens: bfloat16 [384, 5120], P(('dp', 'expert')), may hold values from -6 to 6
- router_weight: bfloat16 [384], P(('dp', 'expert')), may hold values from 0.19921875 to 1
- initial_id: int32 [384, 1], P(('dp', 'expert')), may hold values from 0 to 3; in each aligned block of 192 rows (0 to 191, 192 to 383, ...) at most 80 rows name the same one
- group_map: int32 [4], replicated, may hold values from 0 to 1, as said below
- teacher_gate: bfloat16 [5120, 16384], P(None, 'expert'), may hold values from -0.078125 to 0.078125
- teacher_up: bfloat16 [5120, 16384], P(None, 'expert'), may hold values from -0.078125 to 0.078125
- teacher_down: bfloat16 [16384, 5120], P('expert'), may hold values from -0.09375 to 0.09375
- student_gate: bfloat16 [5120, 8192], P(None, 'expert'), may hold values from -0.078125 to 0.078125
- student_up: bfloat16 [5120, 8192], P(None, 'expert'), may hold values from -0.078125 to 0.078125
- student_down: bfloat16 [8192, 5120], P('expert'), may hold values from -0.09375 to 0.09375
Outputs:
- grad_gate: float32 [5120, 8192], P('dp', 'expert')
- grad_up: float32 [5120, 8192], P('dp', 'expert')
- grad_down: float32 [8192, 5120], P('expert', 'dp')
Inputs may be any that keep to these rules, and one draw needn't show every extreme that they name: `initial_id`: in each half of the tokens (rows h * 12 * 16 to (h + 1) * 12 * 16 - 1, h = 0, 1) every initial expert is named by at most 80 tokens, and some expert of some half by exactly 80. `group_map`: every merged expert is named by exactly 2 entries.
All inputs are finite; a program needn't handle non-finite values.
Results may differ from a plain program's by a relative error of at most 0.013.
Values may be sent and summed in bfloat16 or wider, within the bound.
A program may use at most 192 MiB of HBM per device.

v0:
```python
import math

import jax
import jax.numpy as jnp
from jax import lax
from jax.sharding import PartitionSpec as P

F = 4096
E_ORIG = 4
GROUP = 2


def pick_rows(ids, target, capacity):
    count = ids.shape[0]
    member = ids == target
    keys = jnp.where(member, 0, 1).astype(jnp.int32) * count + jnp.arange(count, dtype=jnp.int32)
    order = jnp.argsort(keys)[:capacity]
    live = jnp.sum(member.astype(jnp.int32))
    valid = jnp.arange(capacity, dtype=jnp.int32) < live
    return (order, valid)


def expert_forward(rows, w_gate, w_up):
    gate = jnp.dot(rows, w_gate, preferred_element_type=jnp.float32)
    upper = jnp.dot(rows, w_up, preferred_element_type=jnp.float32)
    hidden = (jax.nn.silu(gate) * upper).astype(jnp.bfloat16)
    return (gate, upper, hidden)


def per_device(
    tokens,
    router_weight,
    initial_id,
    group_map,
    teacher_gate,
    teacher_up,
    teacher_down,
    student_gate,
    student_up,
    student_down,
):
    whole, weights, id_rows = (
        lax.all_gather(tokens, "expert", axis=0, tiled=True),
        lax.all_gather(router_weight, "expert", axis=0, tiled=True),
        lax.all_gather(initial_id, "expert", axis=0, tiled=True),
    )
    ids = id_rows[:, 0]
    weight = weights.astype(jnp.float32)
    half_rows = whole.shape[0]
    total_tokens = half_rows * lax.axis_size("dp")
    capacity = half_rows * 5 // (E_ORIG * 3)
    owner = lax.axis_index("expert")
    teacher_width = teacher_gate.shape[1]
    student_width = student_gate.shape[1]
    teacher_expert = owner * teacher_width // F
    student_expert = owner * student_width // F
    teacher_idx, teacher_valid = pick_rows(ids, teacher_expert, capacity)
    teacher_x = whole[teacher_idx]
    _, _, teacher_hidden = expert_forward(teacher_x, teacher_gate, teacher_up)
    teacher_scale = jnp.where(teacher_valid, -weight[teacher_idx], 0.0)
    teacher_part = (
        jnp.dot(teacher_hidden, teacher_down, preferred_element_type=jnp.float32)
        * teacher_scale[:, None]
    )
    member_keys = jnp.where(group_map == student_expert, 0, 1).astype(
        jnp.int32
    ) * E_ORIG + jnp.arange(E_ORIG, dtype=jnp.int32)
    members = jnp.argsort(member_keys)[:GROUP]
    index_list, valid_list = ([], [])
    for position in range(GROUP):
        picked, valid = pick_rows(ids, members[position], capacity)
        index_list.append(picked)
        valid_list.append(valid)
    student_idx = jnp.concatenate(index_list)
    student_valid = jnp.concatenate(valid_list)
    student_x = whole[student_idx]
    gate, upper, student_hidden = expert_forward(student_x, student_gate, student_up)
    student_scale = jnp.where(student_valid, weight[student_idx], 0.0)
    student_part = (
        jnp.dot(student_hidden, student_down, preferred_element_type=jnp.float32)
        * student_scale[:, None]
    )
    partial_sum = jnp.zeros((half_rows, whole.shape[1]), jnp.float32)
    partial_sum = partial_sum.at[teacher_idx].add(teacher_part).at[student_idx].add(student_part)
    factor = 1.0 / math.sqrt(total_tokens)
    mismatch = lax.psum(partial_sum, "expert")
    cotangent = (weight[:, None] * mismatch * factor).astype(jnp.bfloat16)
    chosen = jnp.where(student_valid[:, None], cotangent[student_idx], jnp.zeros((), jnp.bfloat16))
    dhidden = jnp.dot(chosen, student_down.T, preferred_element_type=jnp.float32)
    sigma = jax.nn.sigmoid(gate)
    dgate = (dhidden * upper * sigma * (1.0 + gate * (1.0 - sigma))).astype(jnp.bfloat16)
    dup = (dhidden * jax.nn.silu(gate)).astype(jnp.bfloat16)
    gate_grad = jnp.dot(student_x.T, dgate, preferred_element_type=jnp.float32)
    up_grad = jnp.dot(student_x.T, dup, preferred_element_type=jnp.float32)
    down_grad = jnp.dot(student_hidden.T, chosen, preferred_element_type=jnp.float32)
    return (
        lax.psum_scatter(
            gate_grad.astype(jnp.bfloat16), "dp", scatter_dimension=0, tiled=True
        ).astype(jnp.float32),
        lax.psum_scatter(
            up_grad.astype(jnp.bfloat16), "dp", scatter_dimension=0, tiled=True
        ).astype(jnp.float32),
        lax.psum_scatter(
            down_grad.astype(jnp.bfloat16), "dp", scatter_dimension=1, tiled=True
        ).astype(jnp.float32),
    )


def solution(mesh):
    placed = (
        P(("dp", "expert"), None),
        P(("dp", "expert")),
        P(("dp", "expert"), None),
        P(),
        P(None, "expert"),
        P(None, "expert"),
        P("expert", None),
        P(None, "expert"),
        P(None, "expert"),
        P("expert", None),
    )
    return jax.shard_map(
        per_device,
        mesh=mesh,
        in_specs=placed,
        out_specs=(P("dp", "expert"), P("dp", "expert"), P("expert", "dp")),
        check_vma=False,
    )
```

profile of v0, /device:TPU:0, one launch (start us, length us, event | category | flops | bytes accessed | tf_op | source)
XLA Modules:
  0.0 362.0 jit_solution(16532827421106698105)
XLA Ops:
  7.2 0.7 all-gather.3.cloned.1.call-update
  8.0 1.2 dynamic-slice
  9.9 0.9 dynamic-update-slice.1
  10.7 43.7 %all-reduce.1 = bf16[192]{0:T(256)(128)(2,1)S(1)} all-reduce(bf16[192]{0:T(256)(128)(2,1)S(1)} %dynamic-update-slice.1), channel_id=1, replica_groups=mesh['dp'=2,'expert'=16] {'expert'}, use_global_device_ids=true, to_apply=%add.1 | all-reduce | flops 192 | bytes 768
  54.4 0.7 fusion.14
  55.1 0.7 sort.62
  55.8 0.7 bitcast_dynamic-update-slice_fusion
  56.6 8.5 %all-reduce = s32[192]{0:T(256)S(1)} all-reduce(s32[192]{0:T(256)S(1)} %bitcast_dynamic-update-slice_fusion), channel_id=1, replica_groups=mesh['dp'=2,'expert'=16] {'expert'}, use_global_device_ids=true, to_apply=%add | all-reduce | flops 192 | bytes 1536
  65.1 0.6 fusion.20
  65.7 2.0 convert_reduce_fusion.2
  67.7 3.2 sort.63
  70.9 3.2 sort.65
  74.1 3.2 sort.64
  77.2 0.1 compare_select_fusion
  77.3 1.6 gather_fusion.3
  79.0 1.3 gather_fusion.2
  80.2 1.3 iota_compare_fusion
  81.5 0.6 compare_select_fusion.2
  82.2 0.1 broadcast_select_fusion.3
  82.2 2.7 reshape.204
  84.9 1.0 gather_fusion.1
  85.9 2.7 gather_fusion
  88.6 4.1 %fusion.22 = f32[160,512]{1,0:T(8,128)S(1)} fusion(bf16[160,5120]{1,0:T(8,128)(2,1)} %gather_fusion, bf16[5120,512]{1,0:T(8,128)(2,1)} %param.17), kind=kOutput, calls=%fused_computation.62 | convolution fusion | flops 838860800 | bytes 7208960 | tf_op jit(solution)/shard_map/dot_general | solution.py:24
  92.8 6.1 %fusion.21 = f32[80,1024]{1,0:T(8,128)S(1)} fusion(bf16[80,5120]{1,0:T(8,128)(2,1)S(1)} %gather_fusion.1, bf16[5120,1024]{1,0:T(8,128)(2,1)} %param.14), kind=kOutput, calls=%fused_computation.61 | convolution fusion | flops 838860800 | bytes 11632640 | tf_op jit(solution)/shard_map/dot_general | solution.py:24
  98.9 1.7 multiply_convert_fusion.3
  100.7 10.8 %convolution_multiply_fusion.1 = f32[80,5120]{1,0:T(8,128)S(1)} fusion(bf16[1024,5120]{1,0:T(8,128)(2,1)} %param.16, f32[80]{0:T(128)S(1)} %compare_select_fusion.2, bf16[80,5120]{1,0:T(8,128)(2,1)S(1)} %gather_fusion.1, bf16[5120,1024]{1,0:T(8,128)(2,1)} %param.15, f32[80,1024]{1,0:T(8,128)S(1)} %fusion.21), kind=kOutput, calls=%fused_computation.11 | convolution fusion | flops 1678622720 | bytes 23757120 | tf_op jit(solution)/shard_map/dot_general | solution.py:62
  111.4 4.7 %scatter_custom_fusion = f32[192,5120]{1,0:T(8,128)} fusion(s32[80]{0:T(128)S(1)} %compare_select_fusion.1, f32[80,5120]{1,0:T(8,128)S(1)} %convolution_multiply_fusion.1, f32[]{:T(128)} %constant.50.clone.1), kind=kCustom, calls=%fused_computation.13 | custom fusion | flops 409600 | bytes 3932164 | tf_op jit(solution)/shard_map/scatter-add | solution.py:84
  116.1 3.6 convolution_multiply_fusion
  119.7 8.5 %scatter_fusion = f32[192,5120]{1,0:T(8,128)} fusion(f32[192,5120]{1,0:T(8,128)} %scatter_custom_fusion, s32[160]{0:T(256)S(1)} %bitcast.28, f32[160,5120]{1,0:T(8,128)S(1)} %convolution_multiply_fusion), kind=kCustom, calls=%fused_computation.6 | custom fusion | flops 819200 | bytes 9831040 | tf_op jit(solution)/shard_map/scatter-add | solution.py:84
  128.3 0.0 reduce-scatter.8.cloned.1.call-start
  128.3 165.3 %all-reduce.4.cloned.1.call-done = f32[192,5120]{1,0:T(8,128)} async-done(((f32[192,5120]{1,0:T(8,128)}), f32[192,5120]{1,0:T(8,128)}) %all-reduce.4.cloned.1.call-update) | async-done | bytes 3932176 | tf_op jit(solution)/shard_map/psum | solution.py:86
  293.7 2.5 multiply_convert_fusion
  296.2 2.7 gather_fusion.4
  298.9 5.4 %convolution_convert_fusion = bf16[512,5120]{1,0:T(8,128)(2,1)} fusion(bf16[160,512]{1,0:T(8,128)(2,1)S(1)} %get-tuple-element.21, bf16[160,5120]{1,0:T(8,128)(2,1)} %gather_fusion.4, pred[160]{0:T(512)(128)(4,1)S(1)} %get-tuple-element.15), kind=kOutput, calls=%fused_computation.7 | convolution fusion | flops 842301440 | bytes 7045280 | tf_op jit(solution)/shard_map/dot_general | solution.py:95
  304.3 0.0 reduce-scatter.4.cloned.1.call-start
  304.4 1.3 copy-done.2
  305.7 4.5 %fusion.3 = f32[160,512]{1,0:T(8,128)S(1)} fusion(bf16[512,5120]{1,0:T(8,128)(2,1)} %param.19, bf16[160,5120]{1,0:T(8,128)(2,1)S(1)} %copy-done.2, pred[160]{0:T(512)(128)(4,1)S(1)} %get-tuple-element.15), kind=kOutput, calls=%fused_computation.18 | convolution fusion | flops 839680000 | bytes 7209120 | tf_op jit(solution)/shard_map/dot_general | solution.py:89
  310.2 0.7 copy-done.6
  310.9 4.2 %convolution_convert_fusion.2 = bf16[5120,512]{1,0:T(8,128)(2,1)} fusion(bf16[160,5120]{1,0:T(8,128)(2,1)S(1)} %copy-done.1, f32[160,512]{1,0:T(8,128)S(1)} %copy-done.4, f32[160,512]{1,0:T(8,128)S(1)} %fusion.3, f32[160,512]{1,0:T(8,128)S(1)} %copy-done.8), kind=kOutput, calls=%fused_computation.9 | convolution fusion | flops 842301440 | bytes 7864320 | tf_op jit(solution)/shard_map/dot_general | solution.py:93
  315.1 0.3 reduce-scatter.6.cloned.1.call-start
  315.4 0.7 copy-done.5
  316.1 0.1 copy-done.7
  316.2 4.0 %convolution_convert_fusion.1 = bf16[5120,512]{1,0:T(8,128)(2,1)} fusion(bf16[160,5120]{1,0:T(8,128)(2,1)S(1)} %copy-done.1, f32[160,512]{1,0:T(8,128)S(1)} %copy-done.7, f32[160,512]{1,0:T(8,128)S(1)} %copy-done.5), kind=kOutput, calls=%fused_computation.8 | convolution fusion | flops 841973760 | bytes 7536640 | tf_op jit(solution)/shard_map/dot_general | solution.py:94
  320.2 4.8 %convert_element_type.62 = f32[512,2560]{1,0:T(8,128)} convert(bf16[512,2560]{1,0:T(8,128)(2,1)} %reduce-scatter.8.cloned.1.call-done) | non-fusion elementwise | flops 1310720 | bytes 7864320 | tf_op jit(solution)/shard_map/convert_element_type | solution.py:105
  325.0 9.0 %reduce-scatter.4.cloned.1.call-done = bf16[2560,512]{1,0:T(8,128)(2,1)} async-done(((bf16[5120,512]{1,0:T(8,128)(2,1)}), bf16[2560,512]{1,0:T(8,128)(2,1)}) %reduce-scatter.4.cloned.1.call-update) | async-done | bytes 2621456 | tf_op jit(solution)/shard_map/reduce_scatter | solution.py:97
  334.0 4.8 %convert_element_type.57 = f32[2560,512]{1,0:T(8,128)} convert(bf16[2560,512]{1,0:T(8,128)(2,1)} %reduce-scatter.4.cloned.1.call-done) | non-fusion elementwise | flops 1310720 | bytes 7864320 | tf_op jit(solution)/shard_map/convert_element_type | solution.py:99
  338.9 11.8 %reduce-scatter.6.cloned.1.call-done = bf16[2560,512]{1,0:T(8,128)(2,1)} async-done(((bf16[5120,512]{1,0:T(8,128)(2,1)}), bf16[2560,512]{1,0:T(8,128)(2,1)}) %reduce-scatter.6.cloned.1.call-update) | async-done | bytes 2621456 | tf_op jit(solution)/shard_map/reduce_scatter | solution.py:100
  350.7 4.8 %convert_element_type.60 = f32[2560,512]{1,0:T(8,128)} convert(bf16[2560,512]{1,0:T(8,128)(2,1)} %reduce-scatter.6.cloned.1.call-done) | non-fusion elementwise | flops 1310720 | bytes 7864320 | tf_op jit(solution)/shard_map/convert_element_type | solution.py:102
  (38 shorter events, 0.2 us)
Async XLA Ops:
  7.2 75.1 %all-gather.3.cloned.1.call-start = ((), (), s32[]{:S(2)}) async-start(), calls=%async_computation.7 | async-start | bytes 2785280 | tf_op jit(solution)/shard_map/all_gather | solution.py:43
  7.9 285.8 %all-reduce.4.cloned.1.call-start = ((), (), s32[]{:S(2)}) async-start(), calls=%async_computation.3 | async-start | bytes 7864320 | tf_op jit(solution)/shard_map/psum | solution.py:86
  88.6 10.3 %slice-start = ((s8[5242880]{0:T(1024)(128)(4,1)}), s8[4194304]{0:T(1024)(128)(4,1)S(1)}, s32[]{:S(2)}) async-start(s8[5242880]{0:T(1024)(128)(4,1)} %bitcast.29), calls=%async_computation.8 | async-start | bytes 8388608
  92.7 6.1 %copy-start.3 = (f32[160,512]{1,0:T(8,128)}, f32[160,512]{1,0:T(8,128)S(1)}, u32[]{:S(2)}) copy-start(f32[160,512]{1,0:T(8,128)S(1)} %fusion.22) | copy-start | bytes 983044
  92.8 6.1 %copy-start = (bf16[160,5120]{1,0:T(8,128)(2,1)S(1)}, bf16[160,5120]{1,0:T(8,128)(2,1)}, u32[]{:S(2)}) copy-start(bf16[160,5120]{1,0:T(8,128)(2,1)} %gather_fusion) | copy-start | bytes 4915204
  92.8 6.1 %slice-start.1 = ((s8[5242880]{0:T(1024)(128)(4,1)}), s8[1048576]{0:T(1024)(128)(4,1)S(1)}, s32[]{:S(2)}) async-start(s8[5242880]{0:T(1024)(128)(4,1)} %bitcast.29), calls=%async_computation.9 | async-start | bytes 2097152
  128.3 191.9 %reduce-scatter.8.cloned.1.call-start = ((), (), s32[]{:S(2)}) async-start(), calls=%async_computation.6 | async-start | bytes 7864320 | tf_op jit(solution)/shard_map/reduce_scatter | solution.py:103
  304.3 1.4 copy-start.2
  304.3 6.6 %copy-start.1 = (bf16[160,5120]{1,0:T(8,128)(2,1)S(1)}, bf16[160,5120]{1,0:T(8,128)(2,1)}, u32[]{:S(2)}) copy-start(bf16[160,5120]{1,0:T(8,128)(2,1)} %gather_fusion) | copy-start | bytes 4915204
  304.3 29.7 %reduce-scatter.4.cloned.1.call-start = ((), (), s32[]{:S(2)}) async-start(), calls=%async_computation.4 | async-start | bytes 7864320 | tf_op jit(solution)/shard_map/reduce_scatter | solution.py:97
  305.7 5.2 %copy-start.4 = (f32[160,512]{1,0:T(8,128)S(1)}, f32[160,512]{1,0:T(8,128)}, u32[]{:S(2)}) copy-start(f32[160,512]{1,0:T(8,128)} %copy-done.3) | copy-start | bytes 983044
  305.7 5.2 %copy-start.8 = (f32[160,512]{1,0:T(8,128)S(1)}, f32[160,512]{1,0:T(8,128)}, u32[]{:S(2)}) copy-start(f32[160,512]{1,0:T(8,128)} %get-tuple-element.22) | copy-start | bytes 983044
  310.2 0.7 copy-start.6
  315.1 1.0 copy-start.5
  315.1 1.1 copy-start.7
  315.1 35.5 %reduce-scatter.6.cloned.1.call-start = ((), (), s32[]{:S(2)}) async-start(), calls=%async_computation.5 | async-start | bytes 7864320 | tf_op jit(solution)/shard_map/reduce_scatter | solution.py:100
Sparse Core Ops, SparseCore 0:
  10.7 67.7 all-gather.2
  128.4 165.2 all-reduce.3
  304.4 12.2 reduce-scatter.7
  319.5 14.4 reduce-scatter.3
  336.2 14.4 reduce-scatter.5
where the time goes:
time: 363 us; the launch traced here: 362 us
  waiting for transfers between devices  187 us (52%)
  blocking collectives  52.2 us (14%)
  other arithmetic  45.3 us (12%)
  matrix products  44.3 us (12%)
  local copies, waits for them, and re-layouts  18.3 us (5%)
  between operations  14.7 us (4%)
    psum x1, waiting for transfers between devices, per_device(): mismatch = lax.psum(partial_sum, 'expert')  165 us
    unnamed x2, blocking collectives  52.2 us
    convert_element_type x3, other arithmetic, per_device(): return (lax.psum_scatter(gate_grad.astype(jnp.bfloat16), 'dp', scatter_di...  14.5 us
    scatter-add x2, other arithmetic, per_device(): partial_sum.at[teacher_idx].add(teacher_part).at[student_idx]  13.2 us
    reduce_scatter x1, waiting for transfers between devices, per_device(): lax.psum_scatter(up_grad.astype(jnp.bfloat16), 'dp', scatter_dimension=0,...  11.8 us
    dot_general x1, matrix products, per_device(): jnp.dot(teacher_hidden, teacher_down, preferred_element_type=jnp.float32)  10.8 us
    dot_general x2, matrix products, expert_forward(): gate = jnp.dot(rows, w_gate, preferred_element_type=jnp.float32)  10.2 us
    sort x3, other arithmetic, pick_rows(): order = jnp.argsort(keys)[:capacity]  9.51 us
  transfers between devices with their start and end apart: 5, of which 3 were waited for; matrix products, arithmetic and copies ran while one was open for 12% of the time, Pallas kernels for 0%

commit v1 on v0

v1 whole, which is shorter than its diff:
```python
import functools
import math

import jax
import jax.numpy as jnp
from jax import lax
from jax.experimental import pallas as pl
from jax.experimental.pallas import tpu as pltpu
from jax.sharding import PartitionSpec as P

F = 4096
SLOT = 16
EXTRA = 128
MESH = pl.DeviceIdType.MESH
Y, X, Z = 0, 1, 2
ORDERS = ((Z, X, Y), (Z, Y, X), (Z, X, Y), (Z, Y, X))
bf16, f32 = jnp.bfloat16, jnp.float32


def bounds_of(width):
    step = width // 128 // len(ORDERS) * 128
    edges = [step * i for i in range(len(ORDERS))] + [width]
    return list(zip(edges[:-1], edges[1:]))


def kernel(sizes, tok, width, *refs):
    (x_ref, tg_h, tu_h, td_h, sg_h, su_h, sd_h) = refs[:7]
    (got_gate, got_up, got_down, xg_o, cot_o, dg_o, du_o, sh_o) = refs[7:15]
    (tg, tu, td, sg, su, sd, xg, part, cot, gate, up, th, sh, dg, du) = refs[15:30]
    (w_sem, o_sem, g_send, g_recv, a_send, a_recv, c_send, c_recv, r_send, r_recv) = refs[30:40]
    rbufs = refs[40:]
    sy, sx, sz = sizes
    count = sy * sx * sz
    rows = count * SLOT
    y_tile = max(1, 256 // (sx * sz * SLOT))
    m_rows = y_tile * sx * sz * SLOT
    m_steps = sy // y_tile
    tw, sw = tg.shape[1], sg.shape[1]
    half = width // 2

    me = lax.axis_index("expert")
    core = lax.axis_index("dp")
    at = [lax.rem(me // sx, sy), lax.rem(me, sx), me // (sx * sy)]

    def number(pos):
        return (pos[Z] * sy + pos[Y]) * sx + pos[X]

    def moved(axis, k):
        pos = list(at)
        pos[axis] = lax.rem(at[axis] + k + sizes[axis], sizes[axis])
        return pos

    loads = []
    for i, (src, dst) in enumerate(
        ((tg_h, tg), (tu_h, tu), (sg_h, sg), (su_h, su), (td_h, td), (sd_h, sd))
    ):
        loads.append(pltpu.make_async_copy(src, dst, w_sem.at[i]))

    barrier = pltpu.get_barrier_semaphore()
    for axis in (Y, X, Z):
        for k in range(1, sizes[axis]):
            pl.semaphore_signal(
                barrier, inc=1, device_id={"expert": number(moved(axis, k))}, device_id_type=MESH
            )
    pl.semaphore_signal(barrier, inc=1, device_id={"dp": 1 - core}, device_id_type=MESH)
    xg[pl.ds(at[Y], 1), pl.ds(at[X], 1), pl.ds(at[Z], 1)] = x_ref[...].reshape(1, 1, 1, SLOT, -1)
    pl.semaphore_wait(barrier, sy + sx + sz - 2)

    def region(pos, done):
        return tuple(
            pl.ds(0, sizes[a]) if a in done else pl.ds(pos[a], 1) for a in (Y, X, Z)
        )

    def view(ref, pos, done, cols):
        return ref.at[region(pos, done) + (pl.ds(0, SLOT), pl.ds(cols[0], cols[1] - cols[0]))]

    def spread(buf, send, recv, c, cols, stage):
        axis, done = ORDERS[c][stage], ORDERS[c][:stage]
        copies = []
        for k in range(1, sizes[axis]):
            mine = view(buf, at, done, cols)
            out = pltpu.make_async_remote_copy(
                src_ref=mine, dst_ref=mine,
                send_sem=send.at[c, stage, k - 1], recv_sem=recv.at[c, stage, k - 1],
                device_id={"expert": number(moved(axis, k))}, device_id_type=MESH,
            )
            theirs = view(buf, moved(axis, -k), done, cols)
            came = pltpu.make_async_remote_copy(
                src_ref=theirs, dst_ref=theirs,
                send_sem=send.at[c, stage, k - 1], recv_sem=recv.at[c, stage, k - 1],
                device_id={"expert": number(moved(axis, -k))}, device_id_type=MESH,
            )
            copies.append((out, came))
        return copies

    def begin(copies):
        for out, _ in copies:
            out.start()

    def arrive(copies):
        for _, came in copies:
            came.wait_recv()

    def left(copies):
        for out, _ in copies:
            out.wait_send()

    x_cols = bounds_of(width + EXTRA)
    plan = [[spread(xg, a_send, a_recv, c, x_cols[c], s) for s in range(3)] for c in range(len(ORDERS))]
    for c in range(len(ORDERS)):
        begin(plan[c][0])
    for load in loads:
        load.start()
    for s in (1, 2):
        for c in range(len(ORDERS)):
            arrive(plan[c][s - 1])
            begin(plan[c][s])
    for c in range(len(ORDERS)):
        arrive(plan[c][2])
    outs = [pltpu.make_async_copy(xg, xg_o, o_sem.at[0])]
    outs[0].start()

    def tile_of(ref, m, cols):
        got = ref[pl.ds(m * y_tile, y_tile), :, :, :, cols]
        return got.reshape(m_rows, got.shape[-1])

    def row_ds(m):
        return pl.ds(pl.multiple_of(m * m_rows, m_rows), m_rows)

    def facts(m):
        extra = tile_of(xg, m, pl.ds(width, EXTRA)).astype(f32)
        weight, ids, merged = extra[:, 0:1], extra[:, 1:2], extra[:, 2:3]
        t_own = (me * tw // F).astype(f32)
        s_own = (me * sw // F).astype(f32)
        return (
            jnp.where(ids == t_own, -weight, 0.0),
            jnp.where(merged == s_own, weight, 0.0),
            jnp.where(merged == s_own, 1.0, 0.0),
        )

    def col_ds(j, size):
        return pl.ds(pl.multiple_of(j * size, size), size)

    t_tile, s_tile = min(256, tw), min(256, sw)
    for load in loads[:2]:
        load.wait()

    @pl.loop(0, m_steps)
    def _(m):
        @pl.loop(0, tw // t_tile)
        def _(j):
            cols = col_ds(j, t_tile)
            x = tile_of(xg, m, pl.ds(0, width))
            g = jnp.dot(x, tg[:, cols], preferred_element_type=f32)
            u = jnp.dot(x, tu[:, cols], preferred_element_type=f32)
            th[row_ds(m), cols] = (g * jax.nn.sigmoid(g) * u).astype(bf16)

    for load in loads[2:4]:
        load.wait()

    @pl.loop(0, m_steps)
    def _(m):
        @pl.loop(0, sw // s_tile)
        def _(j):
            cols = col_ds(j, s_tile)
            _, _, keep = facts(m)
            x = tile_of(xg, m, pl.ds(0, width))
            g = jnp.dot(x, sg[:, cols], preferred_element_type=f32)
            u = jnp.dot(x, su[:, cols], preferred_element_type=f32)
            gate[row_ds(m), cols] = g
            up[row_ds(m), cols] = u
            sh[row_ds(m), cols] = (g * jax.nn.sigmoid(g) * u * keep).astype(bf16)

    for load in loads[4:]:
        load.wait()

    def fold(c, cols, stage):
        axis = ORDERS[c][2 - stage]
        done = ORDERS[c][: 2 - stage]
        buf = rbufs[3 * c + stage]
        copies = []
        for k in range(1, sizes[axis]):
            out = pltpu.make_async_remote_copy(
                src_ref=view(part, moved(axis, k), done, cols), dst_ref=buf.at[k - 1],
                send_sem=r_send.at[c, stage, k - 1], recv_sem=r_recv.at[c, stage, k - 1],
                device_id={"expert": number(moved(axis, k))}, device_id_type=MESH,
            )
            copies.append((out, out))
        return copies

    def total(c, cols, stage):
        done = ORDERS[c][: 2 - stage]
        place = region(at, done) + (pl.ds(0, SLOT), pl.ds(cols[0], cols[1] - cols[0]))
        value = part[place].astype(f32)
        for k in range(rbufs[3 * c + stage].shape[0]):
            value = value + rbufs[3 * c + stage][k].astype(f32)
        return place, value

    d_cols = bounds_of(width)
    folds = [[fold(c, d_cols[c], s) for s in range(3)] for c in range(len(ORDERS))]
    shares = [[spread(cot, c_send, c_recv, c, d_cols[c], s) for s in range(3)] for c in range(len(ORDERS))]
    for c, (low, high) in enumerate(d_cols):
        @pl.loop(0, m_steps)
        def _(m):
            @pl.loop(0, (high - low) // 256)
            def _(j):
                cols = pl.ds(pl.multiple_of(low + j * 256, 256), 256)
                t_scale, s_scale, _ = facts(m)
                value = jnp.dot(th[row_ds(m), :], td[:, cols], preferred_element_type=f32) * t_scale
                value += jnp.dot(sh[row_ds(m), :], sd[:, cols], preferred_element_type=f32) * s_scale
                part[pl.ds(m * y_tile, y_tile), :, :, :, cols] = value.astype(bf16).reshape(
                    y_tile, sx, sz, SLOT, 256
                )
        begin(folds[c][0])
    for s in (1, 2):
        for c in range(len(ORDERS)):
            arrive(folds[c][s - 1])
            place, value = total(c, d_cols[c], s - 1)
            part[place] = value.astype(bf16)
            begin(folds[c][s])
    own_weight = xg[region(at, ()) + (pl.ds(0, SLOT), pl.ds(width, EXTRA))].astype(f32)[..., 0:1]
    factor = 1.0 / math.sqrt(tok * count * 2)
    for c in range(len(ORDERS)):
        arrive(folds[c][2])
        place, value = total(c, d_cols[c], 2)
        cot[place] = (own_weight * value * factor).astype(bf16)
        begin(shares[c][0])
    for s in (1, 2):
        for c in range(len(ORDERS)):
            arrive(shares[c][s - 1])
            begin(shares[c][s])
    for c in range(len(ORDERS)):
        arrive(shares[c][2])
    outs.append(pltpu.make_async_copy(cot, cot_o, o_sem.at[1]))
    outs[1].start()

    other = 1 - core
    turned = (((0,), (0,)), ((), ()))

    @pl.loop(0, half // 256)
    def _(i):
        cols = pl.ds(pl.multiple_of(other * half + i * 256, 256), 256)
        value = jnp.zeros((sw, 256), f32)
        for m in range(m_steps):
            value += lax.dot_general(
                sh[row_ds(m), :], tile_of(cot, m, cols), turned, preferred_element_type=f32
            )
        td[pl.ds(0, sw), col_ds(i, 256)] = value.astype(bf16)

    def hand(i, src, dst):
        copy = pltpu.make_async_remote_copy(
            src_ref=src, dst_ref=dst, send_sem=g_send.at[i], recv_sem=g_recv.at[i],
            device_id={"dp": other}, device_id_type=MESH,
        )
        copy.start()
        return copy

    hands = [hand(0, td.at[pl.ds(0, sw), pl.ds(0, half)], got_down)]

    @pl.loop(0, m_steps)
    def _(m):
        @pl.loop(0, sw // s_tile)
        def _(j):
            cols = col_ds(j, s_tile)
            _, _, keep = facts(m)
            dh = lax.dot_general(
                tile_of(cot, m, pl.ds(0, width)), sd[cols, :], (((1,), (1,)), ((), ())),
                preferred_element_type=f32,
            ) * keep
            g, u = gate[row_ds(m), cols], up[row_ds(m), cols]
            s = jax.nn.sigmoid(g)
            dg[row_ds(m), cols] = (dh * u * s * (1.0 + g * (1.0 - s))).astype(bf16)
            du[row_ds(m), cols] = (dh * (g * s)).astype(bf16)

    for i, (src, dst) in enumerate(((dg, dg_o), (du, du_o), (sh, sh_o))):
        outs.append(pltpu.make_async_copy(src, dst, o_sem.at[2 + i]))
        outs[-1].start()

    for number_, (grad, got) in enumerate(((dg, got_gate), (du, got_up))):
        @pl.loop(0, half // 256)
        def _(i):
            cols = pl.ds(pl.multiple_of(other * half + i * 256, 256), 256)
            value = jnp.zeros((256, sw), f32)
            for m in range(m_steps):
                value += lax.dot_general(
                    tile_of(xg, m, cols), grad[row_ds(m), :], turned, preferred_element_type=f32
                )
            tg[col_ds(i, 256), pl.ds(number_ * sw, sw)] = value.astype(bf16)
        hands.append(hand(1 + number_, tg.at[pl.ds(0, half), pl.ds(number_ * sw, sw)], got))

    for c in range(len(ORDERS)):
        for s in range(3):
            left(plan[c][s])
            left(folds[c][s])
            left(shares[c][s])
    for copy in outs:
        copy.wait()
    for copy in hands:
        copy.wait()


def per_device(
    tokens, router_weight, initial_id, group_map,
    teacher_gate, teacher_up, teacher_down, student_gate, student_up, student_down,
):
    count = lax.axis_size("expert")
    sz = 4
    side = math.isqrt(count // sz)
    sizes = (side, side, sz)
    tok, width = tokens.shape
    half = width // 2
    rows = count * SLOT
    tw, sw = teacher_gate.shape[1], student_gate.shape[1]

    ids = initial_id[:, 0]
    merged = jnp.sum(
        jnp.where(ids[:, None] == jnp.arange(group_map.shape[0])[None, :], group_map[None, :], 0), axis=1
    )
    lane = jnp.arange(EXTRA)[None, :]
    extra = jnp.where(
        lane == 0, router_weight[:, None],
        jnp.where(lane == 1, ids[:, None].astype(bf16), merged[:, None].astype(bf16)),
    ).astype(bf16)
    block = jnp.pad(jnp.concatenate([tokens, extra], axis=1), ((0, SLOT - tok), (0, 0)))

    wide = sizes + (SLOT, width + EXTRA)
    narrow = sizes + (SLOT, width)
    out_shape = (
        jax.ShapeDtypeStruct((half, sw), bf16),
        jax.ShapeDtypeStruct((half, sw), bf16),
        jax.ShapeDtypeStruct((sw, half), bf16),
        jax.ShapeDtypeStruct(wide, bf16),
        jax.ShapeDtypeStruct(narrow, bf16),
        jax.ShapeDtypeStruct((rows, sw), bf16),
        jax.ShapeDtypeStruct((rows, sw), bf16),
        jax.ShapeDtypeStruct((rows, sw), bf16),
    )
    scratch = [
        pltpu.VMEM((width, tw), bf16), pltpu.VMEM((width, tw), bf16), pltpu.VMEM((tw, width), bf16),
        pltpu.VMEM((width, sw), bf16), pltpu.VMEM((width, sw), bf16), pltpu.VMEM((sw, width), bf16),
        pltpu.VMEM(wide, bf16), pltpu.VMEM(narrow, bf16), pltpu.VMEM(narrow, bf16),
        pltpu.VMEM((rows, sw), f32), pltpu.VMEM((rows, sw), f32),
        pltpu.VMEM((rows, tw), bf16), pltpu.VMEM((rows, sw), bf16),
        pltpu.VMEM((rows, sw), bf16), pltpu.VMEM((rows, sw), bf16),
        pltpu.SemaphoreType.DMA((6,)), pltpu.SemaphoreType.DMA((5,)),
        pltpu.SemaphoreType.DMA((3,)), pltpu.SemaphoreType.DMA((3,)),
    ] + [pltpu.SemaphoreType.DMA((len(ORDERS), 3, 3))] * 6
    for order, (low, high) in zip(ORDERS, bounds_of(width)):
        for stage in range(3):
            axis, done = order[2 - stage], order[: 2 - stage]
            dims = tuple(sizes[a] if a in done else 1 for a in (Y, X, Z))
            scratch.append(pltpu.VMEM((sizes[axis] - 1,) + dims + (SLOT, high - low), bf16))
    hbm = pl.BlockSpec(memory_space=pl.ANY)
    got_gate, got_up, got_down, xg, cot, dg, du, sh = pl.pallas_call(
        functools.partial(kernel, sizes, tok, width),
        out_shape=out_shape,
        in_specs=[pl.BlockSpec(memory_space=pltpu.VMEM)] + [hbm] * 6,
        out_specs=[hbm] * 8,
        scratch_shapes=scratch,
        compiler_params=pltpu.CompilerParams(
            collective_id=0, has_side_effects=True, vmem_limit_bytes=63 * 2**20
        ),
    )(block, teacher_gate, teacher_up, teacher_down, student_gate, student_up, student_down)

    start = lax.axis_index("dp") * half
    x_own = lax.dynamic_slice_in_dim(xg.reshape(rows, width + EXTRA), start, half, 1)
    c_own = lax.dynamic_slice_in_dim(cot.reshape(rows, width), start, half, 1)
    turned = (((0,), (0,)), ((), ()))

    def own(a, b, got):
        return lax.dot_general(a, b, turned, preferred_element_type=f32) + got.astype(f32)

    return own(x_own, dg, got_gate), own(x_own, du, got_up), own(sh, c_own, got_down)


def solution(mesh):
    placed = (
        P(("dp", "expert"), None),
        P(("dp", "expert")),
        P(("dp", "expert"), None),
        P(),
        P(None, "expert"),
        P(None, "expert"),
        P("expert", None),
        P(None, "expert"),
        P(None, "expert"),
        P("expert", None),
    )
    return jax.shard_map(
        per_device,
        mesh=mesh,
        in_specs=placed,
        out_specs=(P("dp", "expert"), P("dp", "expert"), P("expert", "dp")),
        check_vma=False,
    )
```

time: 363 us -> 153 us (0.42)
  waiting for transfers between devices: 187 us -> 0 us
  Pallas kernels: 0 us -> 133 us
  blocking collectives: 52.2 us -> 0 us
  other arithmetic: 45.3 us -> 3.77 us
  matrix products: 44.3 us -> 13.6 us
  local copies, waits for them, and re-layouts: 18.3 us -> 0.02 us
  between operations: 14.7 us -> 0.69 us
    psum x1 -> x0, waiting for transfers between devices: 165 us -> none  [per_device(): mismatch = lax.psum(partial_sum, 'expert')]
    pallas_call x0 -> x1, Pallas kernels: none -> 133 us  [per_device(): pl.pallas_call(functools.partial(kernel, sizes, tok, width), out_shape=ou...]
    unnamed x2 -> x0, blocking collectives: 52.2 us -> none
    dot_general x9 -> x3, matrix products: 44.3 us -> 13.6 us  [own(): lax.dot_general(a, b, turned, preferred_element_type=f32) + got.astype(f32)]
    reduce_scatter x3 -> x0, waiting for transfers between devices: 20.8 us -> none  [the longest x1 11.8 us: per_device(): lax.psum_scatter(up_grad.astype(jnp.bfloat16), 'dp', scatter_dimension=0,...]
    convert_element_type x5 -> x1, other arithmetic: 17 us -> 0.01 us  [per_device(): merged[:, None].astype(bf16)]
    scatter-add x2 -> x0, other arithmetic: 13.2 us -> none  [per_device(): partial_sum.at[teacher_idx].add(teacher_part).at[student_idx]]
    sort x4 -> x0, other arithmetic: 10.3 us -> none  [the longest x3 9.51 us: pick_rows(): order = jnp.argsort(keys)[:capacity]]
  transfers between devices with their start and end apart: 5 -> 0, of which waited for: 3 -> 0; matrix products, arithmetic and copies ran while one was open for 12% -> 0% of each run, Pallas kernels for 0% -> 0%
where the time goes in v1:
time: 153 us; the launch traced here: 151 us
  Pallas kernels  133 us (87%)
  matrix products  13.6 us (9%)
  other arithmetic  3.77 us (2%)
    pallas_call x1, Pallas kernels, per_device(): pl.pallas_call(functools.partial(kernel, sizes, tok, width), out_shape=ou...  133 us
    dot_general x3, matrix products, own(): lax.dot_general(a, b, turned, preferred_element_type=f32) + got.astype(f32)  13.6 us

profile of v1, /device:TPU:0, one launch (start us, length us, event | category | flops | bytes accessed | tf_op | source)
XLA Modules:
  0.0 151.2 jit_solution(10416516133723577967)
XLA Ops:
  0.6 0.8 select_reduce_fusion
  1.4 0.7 convert_bitcast_fusion
  2.1 0.7 select_select_fusion
  2.8 1.6 %fusion.5.refs_0_ = bf16[16,5248]{1,0:T(8,128)(2,1)} fusion(bf16[12,128]{1,0:T(8,128)(2,1)S(1)} %select_select_fusion, bf16[12,5120]{1,0:T(8,128)(2,1)} %param.10), kind=kLoop, calls=%fused_computation.9 | loop fusion | flops 587776 | bytes 293888 | tf_op jit(solution)/shard_map/concatenate | solution.py:324
  4.4 133.2 %shard_map.121 = (bf16[2560,512]{1,0:T(8,128)(2,1)}, bf16[2560,512]{1,0:T(8,128)(2,1)}, bf16[512,2560]{1,0:T(8,128)(2,1)}, bf16[2,2,4,16,5248]{4,3,2,1,0:T(8,128...) custom-call(bf16[16,5248]{1,0:T(8,128)(2,1)} %fusion.5.refs_0_, ...), custom_call_target="tpu_custom_call" | custom-call | tf_op jit(solution)/shard_map/pallas_call | solution.py:354
  137.6 0.0 copy-start
  137.6 0.0 copy-start.3
  137.6 5.6 %convert_add_fusion.1 = f32[2560,512]{1,0:T(8,128)} fusion(bf16[2560,512]{1,0:T(8,128)(2,1)} %get-tuple-element.15, bf16[256,512]{1,0:T(8,128)(2,1)} %get-tuple-element.14, bf16[256,5248]{1,0:T(8,128)(2,1)} %bitcast.8, s32[]{:T(128)S(6)} %select_n.21), kind=kOutput, calls=%fused_computation.1 | convolution fusion | flops 673710080 | bytes 9437188 | tf_op jit(solution)/shard_map/dot_general | solution.py:371
  143.3 0.0 copy-done
  143.3 0.0 copy-done.3
  143.3 0.0 copy-start.1
  143.3 0.0 copy-start.2
  143.3 0.0 copy-start.4
  143.3 4.7 %convert_add_fusion.2 = f32[2560,512]{1,0:T(8,128)} fusion(bf16[2560,512]{1,0:T(8,128)(2,1)S(1)} %copy-done, bf16[256,512]{1,0:T(8,128)(2,1)S(1)} %copy-done.3, bf16[256,5248]{1,0:T(8,128)(2,1)} %bitcast.9, s32[]{:T(128)S(6)} %select_n.21), kind=kOutput, calls=%fused_computation.2 | convolution fusion | flops 673710080 | bytes 9437188 | tf_op jit(solution)/shard_map/dot_general | solution.py:371
  148.0 0.0 copy-done.1
  148.0 0.0 copy-done.2
  148.0 0.0 copy-done.4
  148.0 3.2 %convert_add_fusion = f32[512,2560]{1,0:T(8,128)} fusion(bf16[512,2560]{1,0:T(8,128)(2,1)S(1)} %copy-done.1, bf16[256,512]{1,0:T(8,128)(2,1)S(1)} %copy-done.4, bf16[256,5120]{1,0:T(8,128)(2,1)S(1)} %bitcast.10, s32[]{:T(128)S(6)} %select_n.22), kind=kOutput, calls=%fused_computation | convolution fusion | flops 673710080 | bytes 9437188 | tf_op jit(solution)/shard_map/dot_general | solution.py:371
  (2 shorter events, 0.0 us)
Async XLA Ops:
  137.6 5.6 %copy-start = (bf16[2560,512]{1,0:T(8,128)(2,1)S(1)}, bf16[2560,512]{1,0:T(8,128)(2,1)}, u32[]{:S(2)}) copy-start(bf16[2560,512]{1,0:T(8,128)(2,1)} %get-tuple-element.13) | copy-start | bytes 7864324
  137.6 5.6 %copy-start.3 = (bf16[256,512]{1,0:T(8,128)(2,1)S(1)}, bf16[256,512]{1,0:T(8,128)(2,1)}, u32[]{:S(2)}) copy-start(bf16[256,512]{1,0:T(8,128)(2,1)} %get-tuple-element.12) | copy-start | bytes 786436
  143.3 4.7 %copy-start.1 = (bf16[512,2560]{1,0:T(8,128)(2,1)S(1)}, bf16[512,2560]{1,0:T(8,128)(2,1)}, u32[]{:S(2)}) copy-start(bf16[512,2560]{1,0:T(8,128)(2,1)} %get-tuple-element.18) | copy-start | bytes 7864324
  143.3 4.7 %copy-start.2 = (bf16[2,2,4,16,5120]{4,3,2,1,0:T(8,128)(2,1)S(1)}, bf16[2,2,4,16,5120]{4,3,2,1,0:T(8,128)(2,1)}, u32[]{:S(2)}) copy-start(bf16[2,2,4,16,5120]{4,3,2,1,0:T(8,128)(2,1)} %get-tuple-element.17) | copy-start | bytes 7864324
  143.3 4.7 %copy-start.4 = (bf16[256,512]{1,0:T(8,128)(2,1)S(1)}, bf16[256,512]{1,0:T(8,128)(2,1)}, u32[]{:S(2)}) copy-start(bf16[256,512]{1,0:T(8,128)(2,1)} %get-tuple-element.16) | copy-start | bytes 786436

commit v2 on v1

v2 whole, which is shorter than its diff:
```python
import functools
import math

import jax
import jax.numpy as jnp
from jax import lax
from jax.experimental import pallas as pl
from jax.experimental.pallas import tpu as pltpu
from jax.sharding import PartitionSpec as P

F = 4096
SLOT = 16
EXTRA = 128
MESH = pl.DeviceIdType.MESH
Y, X, Z = 0, 1, 2
ORDERS = ((Z, X, Y), (Z, Y, X), (Z, X, Y), (Z, Y, X), (Z, X, Y))
PARTS = len(ORDERS)
bf16, f32 = jnp.bfloat16, jnp.float32


def pieces(width):
    step = width * 3 // 4 // PARTS
    return [(step * i, step * (i + 1)) for i in range(PARTS)]


def kernel(sizes, tok, width, *refs):
    (x_ref, tg_h, tu_h, td_h, sg_h, su_h, sd_h) = refs[:7]
    (got_gate, got_up, got_down, xg_o, cot_o, dg_o, du_o, sh_o) = refs[7:15]
    (tg, tu, td, sg, su, sd, xg, part, cot, gate, up, th, sh, dg, du, t_gate, t_up) = refs[15:32]
    (w_sem, o_sem, g_send, g_recv, a_send, a_recv, c_send, c_recv, r_send, r_recv) = refs[32:42]
    rbufs = refs[42:]
    sy, sx, sz = sizes
    count = sy * sx * sz
    rows = count * SLOT
    y_tile = max(1, 256 // (sx * sz * SLOT))
    m_rows = y_tile * sx * sz * SLOT
    m_steps = sy // y_tile
    tw, sw = tg.shape[1], sg.shape[1]
    half = width // 2
    sent = width * 3 // 4
    cut = width // 4 // PARTS

    me = lax.axis_index("expert")
    core = lax.axis_index("dp")
    at = [lax.rem(me // sx, sy), lax.rem(me, sx), me // (sx * sy)]

    def number(pos):
        return (pos[Z] * sy + pos[Y]) * sx + pos[X]

    def moved(axis, k):
        pos = list(at)
        pos[axis] = lax.rem(at[axis] + k + sizes[axis], sizes[axis])
        return pos

    loads = []
    for i, (src, dst) in enumerate(
        ((tg_h, tg), (tu_h, tu), (sg_h, sg), (su_h, su), (td_h, td), (sd_h, sd))
    ):
        loads.append(pltpu.make_async_copy(src, dst, w_sem.at[i]))
        loads[-1].start()

    barrier = pltpu.get_barrier_semaphore()
    for axis in (Y, X, Z):
        for k in range(1, sizes[axis]):
            pl.semaphore_signal(
                barrier, inc=1, device_id={"expert": number(moved(axis, k))}, device_id_type=MESH
            )
    pl.semaphore_signal(barrier, inc=1, device_id={"dp": 1 - core}, device_id_type=MESH)
    mine = (pl.ds(at[Y], 1), pl.ds(at[X], 1), pl.ds(at[Z], 1), pl.ds(0, SLOT))
    xg[mine + (pl.ds(0, sent),)] = x_ref[:, pl.ds(0, sent)].reshape(1, 1, 1, SLOT, sent)
    xg[mine + (pl.ds(width, EXTRA),)] = x_ref[:, pl.ds(sent, EXTRA)].reshape(1, 1, 1, SLOT, EXTRA)
    pl.semaphore_wait(barrier, sy + sx + sz - 2)

    def region(pos, done):
        return tuple(
            pl.ds(0, sizes[a]) if a in done else pl.ds(pos[a], 1) for a in (Y, X, Z)
        )

    def view(ref, pos, done, cols):
        return ref.at[region(pos, done) + (pl.ds(0, SLOT), pl.ds(cols[0], cols[1] - cols[0]))]

    def spread(buf, send, recv, c, cols, stage):
        axis, done = ORDERS[c % PARTS][stage], ORDERS[c % PARTS][:stage]
        copies = []
        for k in range(1, sizes[axis]):
            mine = view(buf, at, done, cols)
            out = pltpu.make_async_remote_copy(
                src_ref=mine, dst_ref=mine,
                send_sem=send.at[c, stage, k - 1], recv_sem=recv.at[c, stage, k - 1],
                device_id={"expert": number(moved(axis, k))}, device_id_type=MESH,
            )
            theirs = view(buf, moved(axis, -k), done, cols)
            came = pltpu.make_async_remote_copy(
                src_ref=theirs, dst_ref=theirs,
                send_sem=send.at[c, stage, k - 1], recv_sem=recv.at[c, stage, k - 1],
                device_id={"expert": number(moved(axis, -k))}, device_id_type=MESH,
            )
            copies.append((out, came))
        return copies

    def begin(copies):
        for out, _ in copies:
            out.start()

    def arrive(copies):
        for _, came in copies:
            came.wait_recv()

    def left(copies):
        for out, _ in copies:
            out.wait_send()

    def tile_of(ref, m, cols):
        got = ref[pl.ds(m * y_tile, y_tile), :, :, :, cols]
        return got.reshape(m_rows, got.shape[-1])

    def put_tile(ref, m, cols, value):
        ref[pl.ds(m * y_tile, y_tile), :, :, :, cols] = value.astype(bf16).reshape(
            y_tile, sx, sz, SLOT, value.shape[-1]
        )

    def row_ds(m):
        return pl.ds(pl.multiple_of(m * m_rows, m_rows), m_rows)

    def col_ds(j, size):
        return pl.ds(pl.multiple_of(j * size, size), size)

    def facts(m):
        extra = tile_of(xg, m, pl.ds(width, EXTRA)).astype(f32)
        weight, ids, merged = extra[:, 0:1], extra[:, 1:2], extra[:, 2:3]
        t_own = (me * tw // F).astype(f32)
        s_own = (me * sw // F).astype(f32)
        return (
            jnp.where(ids == t_own, -weight, 0.0),
            jnp.where(merged == s_own, weight, 0.0),
            jnp.where(merged == s_own, 1.0, 0.0),
        )

    cols_of = pieces(width)
    piece = cols_of[0][1]

    def rest_of(c):
        return pl.ds(sent + c * cut, cut)

    def place_in_slot(shape):
        return lax.broadcasted_iota(jnp.int32, shape, 0) % SLOT

    def unpack(ref, c):
        @pl.loop(0, m_steps)
        def _(m):
            where = place_in_slot((m_rows, cut)) // 4
            value = jnp.zeros((m_rows, cut), f32)
            for k in range(3):
                tile = tile_of(ref, m, pl.ds(cols_of[c][0] + k * cut, cut)).astype(f32)
                value = jnp.where(where == k, pltpu.roll(tile, m_rows - (12 - 4 * k), 0), value)
            put_tile(ref, m, rest_of(c), value)

    t_tile, s_tile = min(256, tw), min(256, sw)
    last = PARTS - 1

    def project(c, w_gate, w_up, g_sum, u_sum, hidden, size, tile, masked):
        @pl.loop(0, m_steps)
        def _(m):
            @pl.loop(0, size // tile)
            def _(j):
                cols = col_ds(j, tile)
                first = tile_of(xg, m, pl.ds(cols_of[c][0], piece))
                second = tile_of(xg, m, rest_of(c))

                def product(w):
                    return jnp.dot(
                        first, w[pl.ds(cols_of[c][0], piece), cols], preferred_element_type=f32
                    ) + jnp.dot(second, w[rest_of(c), cols], preferred_element_type=f32)

                g, u = product(w_gate), product(w_up)
                if c > 0:
                    g += g_sum[row_ds(m), cols]
                    u += u_sum[row_ds(m), cols]
                if c < last or masked:
                    g_sum[row_ds(m), cols] = g
                    u_sum[row_ds(m), cols] = u
                if c == last:
                    value = g * jax.nn.sigmoid(g) * u
                    if masked:
                        value = value * facts(m)[2]
                    hidden[row_ds(m), cols] = value.astype(bf16)

    x_cols = cols_of + [(width, width + EXTRA)]
    plan = [[spread(xg, a_send, a_recv, c, x_cols[c], s) for s in range(3)] for c in range(PARTS + 1)]
    begin(plan[PARTS][0])
    for c in range(PARTS):
        begin(plan[c][0])
    turn = [PARTS] + list(range(PARTS))
    for t in range(PARTS + 3):
        if 2 <= t < PARTS + 3:
            c = turn[t - 2]
            arrive(plan[c][1])
            begin(plan[c][2])
        if 0 <= t - 1 < PARTS + 1:
            c = turn[t - 1]
            arrive(plan[c][0])
            begin(plan[c][1])
        if 0 <= t - 3:
            c = turn[t - 3]
            arrive(plan[c][2])
            if c < PARTS:
                unpack(xg, c)
                if c == 0:
                    for load in loads[:4]:
                        load.wait()
                project(c, tg, tu, t_gate, t_up, th, tw, t_tile, False)
                project(c, sg, su, gate, up, sh, sw, s_tile, True)
    c = last
    arrive(plan[c][2])
    unpack(xg, c)
    outs = [pltpu.make_async_copy(xg, xg_o, o_sem.at[0])]
    outs[0].start()
    project(c, tg, tu, t_gate, t_up, th, tw, t_tile, False)
    project(c, sg, su, gate, up, sh, sw, s_tile, True)
    for load in loads[4:]:
        load.wait()

    def fold(c, cols, stage):
        axis = ORDERS[c][2 - stage]
        done = ORDERS[c][: 2 - stage]
        buf = rbufs[3 * c + stage]
        copies = []
        for k in range(1, sizes[axis]):
            out = pltpu.make_async_remote_copy(
                src_ref=view(part, moved(axis, k), done, cols), dst_ref=buf.at[k - 1],
                send_sem=r_send.at[c, stage, k - 1], recv_sem=r_recv.at[c, stage, k - 1],
                device_id={"expert": number(moved(axis, k))}, device_id_type=MESH,
            )
            copies.append((out, out))
        return copies

    def total(c, cols, stage):
        done = ORDERS[c][: 2 - stage]
        place = region(at, done) + (pl.ds(0, SLOT), pl.ds(cols[0], cols[1] - cols[0]))
        value = part[place].astype(f32)
        for k in range(rbufs[3 * c + stage].shape[0]):
            value = value + rbufs[3 * c + stage][k].astype(f32)
        return place, value

    folds = [[fold(c, cols_of[c], s) for s in range(3)] for c in range(PARTS)]
    shares = [[spread(cot, c_send, c_recv, c, cols_of[c], s) for s in range(3)] for c in range(PARTS)]
    factor = 1.0 / math.sqrt(tok * count * 2)

    def differ(c):
        @pl.loop(0, m_steps)
        def _(m):
            t_scale, s_scale, _ = facts(m)

            def tile(cols):
                value = jnp.dot(th[row_ds(m), :], td[:, cols], preferred_element_type=f32) * t_scale
                return value + jnp.dot(
                    sh[row_ds(m), :], sd[:, cols], preferred_element_type=f32
                ) * s_scale

            rest = tile(rest_of(c))
            where = place_in_slot((m_rows, cut))
            for k in range(3):
                cols = pl.ds(cols_of[c][0] + k * cut, cut)
                put_tile(part, m, cols, jnp.where(where >= 12, pltpu.roll(rest, 12 - 4 * k, 0), tile(cols)))

    def finish(c):
        own = xg[mine + (pl.ds(width, EXTRA),)].astype(f32).reshape(SLOT, EXTRA)[:, 0:1]
        own = jnp.broadcast_to(own, (SLOT, cut))
        where = place_in_slot((SLOT, cut))
        weight = jnp.concatenate(
            [jnp.where(where >= 12, pltpu.roll(own, 12 - 4 * k, 0), own) for k in range(3)], axis=1
        )
        place, value = total(c, cols_of[c], 2)
        value = weight * value.reshape(SLOT, piece) * factor
        cot[place] = value.astype(bf16).reshape(1, 1, 1, SLOT, piece)

    def back(c):
        @pl.loop(0, m_steps)
        def _(m):
            @pl.loop(0, sw // s_tile)
            def _(j):
                cols = col_ds(j, s_tile)
                nt = (((1,), (1,)), ((), ()))
                dh = lax.dot_general(
                    tile_of(cot, m, pl.ds(cols_of[c][0], piece)), sd[cols, pl.ds(cols_of[c][0], piece)],
                    nt, preferred_element_type=f32,
                ) + lax.dot_general(
                    tile_of(cot, m, rest_of(c)), sd[cols, rest_of(c)], nt, preferred_element_type=f32
                )
                if c > 0:
                    dh += t_gate[row_ds(m), cols]
                if c < last:
                    t_gate[row_ds(m), cols] = dh
                else:
                    dh = dh * facts(m)[2]
                    g, u = gate[row_ds(m), cols], up[row_ds(m), cols]
                    s = jax.nn.sigmoid(g)
                    dg[row_ds(m), cols] = (dh * u * s * (1.0 + g * (1.0 - s))).astype(bf16)
                    du[row_ds(m), cols] = (dh * (g * s)).astype(bf16)

    for t in range(PARTS + 6):
        if t < PARTS:
            differ(t)
            begin(folds[t][0])
        for late in (5, 4):
            if 0 <= t - late < PARTS:
                arrive(shares[t - late][late - 4])
                begin(shares[t - late][late - 3])
        if 0 <= t - 3 < PARTS:
            arrive(folds[t - 3][2])
            finish(t - 3)
            begin(shares[t - 3][0])
        for late in (2, 1):
            if 0 <= t - late < PARTS:
                c = t - late
                arrive(folds[c][late - 1])
                place, value = total(c, cols_of[c], late - 1)
                part[place] = value.astype(bf16)
                begin(folds[c][late])
        if 0 <= t - 6 < PARTS:
            arrive(shares[t - 6][2])
            unpack(cot, t - 6)
            back(t - 6)
    outs.append(pltpu.make_async_copy(cot, cot_o, o_sem.at[1]))
    outs[1].start()
    for i, (src, dst) in enumerate(((dg, dg_o), (du, du_o), (sh, sh_o))):
        outs.append(pltpu.make_async_copy(src, dst, o_sem.at[2 + i]))
        outs[-1].start()

    other = 1 - core
    turned = (((0,), (0,)), ((), ()))

    def hand(i, src, dst):
        copy = pltpu.make_async_remote_copy(
            src_ref=src, dst_ref=dst, send_sem=g_send.at[i], recv_sem=g_recv.at[i],
            device_id={"dp": other}, device_id_type=MESH,
        )
        copy.start()
        return copy

    hands = []
    for number_, (grad, got) in enumerate(((dg, got_gate), (du, got_up))):
        @pl.loop(0, half // 256)
        def _(i):
            cols = pl.ds(pl.multiple_of(other * half + i * 256, 256), 256)
            value = jnp.zeros((256, sw), f32)
            for m in range(m_steps):
                value += lax.dot_general(
                    tile_of(xg, m, cols), grad[row_ds(m), :], turned, preferred_element_type=f32
                )
            tg[col_ds(i, 256), pl.ds(number_ * sw, sw)] = value.astype(bf16)
        hands.append(hand(1 + number_, tg.at[pl.ds(0, half), pl.ds(number_ * sw, sw)], got))

    @pl.loop(0, half // 256)
    def _(i):
        cols = pl.ds(pl.multiple_of(other * half + i * 256, 256), 256)
        value = jnp.zeros((sw, 256), f32)
        for m in range(m_steps):
            value += lax.dot_general(
                sh[row_ds(m), :], tile_of(cot, m, cols), turned, preferred_element_type=f32
            )
        td[pl.ds(0, sw), col_ds(i, 256)] = value.astype(bf16)

    hands.append(hand(0, td.at[pl.ds(0, sw), pl.ds(0, half)], got_down))

    for s in range(3):
        for c in range(PARTS):
            left(folds[c][s])
            left(shares[c][s])
        for c in range(PARTS + 1):
            left(plan[c][s])
    for copy in outs:
        copy.wait()
    for copy in hands:
        copy.wait()


def per_device(
    tokens, router_weight, initial_id, group_map,
    teacher_gate, teacher_up, teacher_down, student_gate, student_up, student_down,
):
    count = lax.axis_size("expert")
    sz = 4
    side = math.isqrt(count // sz)
    sizes = (side, side, sz)
    tok, width = tokens.shape
    half = width // 2
    rows = count * SLOT
    tw, sw = teacher_gate.shape[1], student_gate.shape[1]

    ids = initial_id[:, 0]
    merged = jnp.sum(
        jnp.where(ids[:, None] == jnp.arange(group_map.shape[0])[None, :], group_map[None, :], 0), axis=1
    )
    lane = jnp.arange(EXTRA)[None, :]
    extra = jnp.where(
        lane == 0, router_weight[:, None],
        jnp.where(lane == 1, ids[:, None].astype(bf16), merged[:, None].astype(bf16)),
    ).astype(bf16)
    extra = jnp.pad(extra, ((0, SLOT - tok), (0, 0)), constant_values=-1)
    sent = width * 3 // 4
    cut = width // 4 // PARTS
    rest = tokens[:, sent:].reshape(3, 4, PARTS, cut).transpose(1, 2, 0, 3).reshape(4, sent)
    block = jnp.concatenate([jnp.concatenate([tokens[:, :sent], rest], axis=0), extra], axis=1)

    wide = sizes + (SLOT, width + EXTRA)
    narrow = sizes + (SLOT, width)
    out_shape = (
        jax.ShapeDtypeStruct((half, sw), bf16),
        jax.ShapeDtypeStruct((half, sw), bf16),
        jax.ShapeDtypeStruct((sw, half), bf16),
        jax.ShapeDtypeStruct(wide, bf16),
        jax.ShapeDtypeStruct(narrow, bf16),
        jax.ShapeDtypeStruct((rows, sw), bf16),
        jax.ShapeDtypeStruct((rows, sw), bf16),
        jax.ShapeDtypeStruct((rows, sw), bf16),
    )
    scratch = [
        pltpu.VMEM((width, tw), bf16), pltpu.VMEM((width, tw), bf16), pltpu.VMEM((tw, width), bf16),
        pltpu.VMEM((width, sw), bf16), pltpu.VMEM((width, sw), bf16), pltpu.VMEM((sw, width), bf16),
        pltpu.VMEM(wide, bf16), pltpu.VMEM(sizes + (SLOT, sent), bf16), pltpu.VMEM(narrow, bf16),
        pltpu.VMEM((rows, sw), f32), pltpu.VMEM((rows, sw), f32),
        pltpu.VMEM((rows, tw), bf16), pltpu.VMEM((rows, sw), bf16),
        pltpu.VMEM((rows, sw), bf16), pltpu.VMEM((rows, sw), bf16),
        pltpu.VMEM((rows, tw), f32), pltpu.VMEM((rows, tw), f32),
        pltpu.SemaphoreType.DMA((6,)), pltpu.SemaphoreType.DMA((5,)),
        pltpu.SemaphoreType.DMA((3,)), pltpu.SemaphoreType.DMA((3,)),
    ] + [pltpu.SemaphoreType.DMA((PARTS + 1, 3, 3))] * 6
    for order, (low, high) in zip(ORDERS, pieces(width)):
        for stage in range(3):
            axis, done = order[2 - stage], order[: 2 - stage]
            dims = tuple(sizes[a] if a in done else 1 for a in (Y, X, Z))
            scratch.append(pltpu.VMEM((sizes[axis] - 1,) + dims + (SLOT, high - low), bf16))
    hbm = pl.BlockSpec(memory_space=pl.ANY)
    got_gate, got_up, got_down, xg, cot, dg, du, sh = pl.pallas_call(
        functools.partial(kernel, sizes, tok, width),
        out_shape=out_shape,
        in_specs=[pl.BlockSpec(memory_space=pltpu.VMEM)] + [hbm] * 6,
        out_specs=[hbm] * 8,
        scratch_shapes=scratch,
        compiler_params=pltpu.CompilerParams(
            collective_id=0, has_side_effects=True, vmem_limit_bytes=63 * 2**20
        ),
    )(block, teacher_gate, teacher_up, teacher_down, student_gate, student_up, student_down)

    start = lax.axis_index("dp") * half
    x_own = lax.dynamic_slice_in_dim(xg.reshape(rows, width + EXTRA), start, half, 1)
    c_own = lax.dynamic_slice_in_dim(cot.reshape(rows, width), start, half, 1)
    turned = (((0,), (0,)), ((), ()))

    def own(a, b, got):
        return lax.dot_general(a, b, turned, preferred_element_type=f32) + got.astype(f32)

    return own(x_own, dg, got_gate), own(x_own, du, got_up), own(sh, c_own, got_down)


def solution(mesh):
    placed = (
        P(("dp", "expert"), None),
        P(("dp", "expert")),
        P(("dp", "expert"), None),
        P(),
        P(None, "expert"),
        P(None, "expert"),
        P("expert", None),
        P(None, "expert"),
        P(None, "expert"),
        P("expert", None),
    )
    return jax.shard_map(
        per_device,
        mesh=mesh,
        in_specs=placed,
        out_specs=(P("dp", "expert"), P("dp", "expert"), P("expert", "dp")),
        check_vma=False,
    )
```

time: 153 us -> 142 us (0.928)
  Pallas kernels: 133 us -> 123 us
  local copies, waits for them, and re-layouts: 0.02 us -> 1.78 us
    pallas_call x1, Pallas kernels: 133 us -> 123 us  [per_device(): pl.pallas_call(functools.partial(kernel, sizes, tok, width), out_shape=ou...]
    slice x0 -> x2, local copies, waits for them, and re-layouts: none -> 1.69 us  [the longest x1 0.91 us: per_device(): tokens[:, :sent]]
where the time goes in v2:
time: 142 us
  Pallas kernels  123 us (87%)
  matrix products  13.5 us (10%)
  other arithmetic  2.84 us (2%)
  local copies, waits for them, and re-layouts  1.78 us (1%)
    pallas_call x1, Pallas kernels, per_device(): pl.pallas_call(functools.partial(kernel, sizes, tok, width), out_shape=ou...  123 us
    dot_general x3, matrix products, own(): lax.dot_general(a, b, turned, preferred_element_type=f32) + got.astype(f32)  13.5 us

profile of v2, /device:TPU:0, one launch (start us, length us, event | category | flops | bytes accessed | tf_op | source)
XLA Modules:
  0.0 141.7 jit_solution(6889307219924651648)
XLA Ops:
  0.6 0.8 select_reduce_fusion
  1.4 0.7 convert_bitcast_fusion
  2.1 0.7 select_select_fusion
  2.8 0.8 slice.7
  3.6 0.1 reshape.34
  3.7 0.9 slice.6
  4.6 0.7 fusion.4.refs_0_
  5.3 122.8 %shard_map.121 = (bf16[2560,512]{1,0:T(8,128)(2,1)}, bf16[2560,512]{1,0:T(8,128)(2,1)}, bf16[512,2560]{1,0:T(8,128)(2,1)}, bf16[2,2,4,16,5248]{4,3,2,1,0:T(8,128...) custom-call(bf16[16,3968]{1,0:T(8,128)(2,1)} %fusion.4.refs_0_, ...), custom_call_target="tpu_custom_call" | custom-call | tf_op jit(solution)/shard_map/pallas_call | solution.py:435
  128.1 0.0 copy-start
  128.1 0.0 copy-start.3
  128.1 5.6 %convert_add_fusion.1 = f32[2560,512]{1,0:T(8,128)} fusion(bf16[2560,512]{1,0:T(8,128)(2,1)} %get-tuple-element.15, bf16[256,512]{1,0:T(8,128)(2,1)} %get-tuple-element.14, bf16[256,5248]{1,0:T(8,128)(2,1)} %bitcast.10, s32[]{:T(128)S(6)} %select_n.21), kind=kOutput, calls=%fused_computation.1 | convolution fusion | flops 673710080 | bytes 9437188 | tf_op jit(solution)/shard_map/dot_general | solution.py:452
  133.7 0.0 copy-done
  133.7 0.0 copy-done.3
  133.7 0.0 copy-start.1
  133.7 0.0 copy-start.2
  133.7 0.0 copy-start.4
  133.7 4.7 %convert_add_fusion.2 = f32[2560,512]{1,0:T(8,128)} fusion(bf16[2560,512]{1,0:T(8,128)(2,1)S(1)} %copy-done, bf16[256,512]{1,0:T(8,128)(2,1)S(1)} %copy-done.3, bf16[256,5248]{1,0:T(8,128)(2,1)} %bitcast.11, s32[]{:T(128)S(6)} %select_n.21), kind=kOutput, calls=%fused_computation.2 | convolution fusion | flops 673710080 | bytes 9437188 | tf_op jit(solution)/shard_map/dot_general | solution.py:452
  138.4 0.0 copy-done.1
  138.4 0.0 copy-done.2
  138.4 0.0 copy-done.4
  138.4 3.2 %convert_add_fusion = f32[512,2560]{1,0:T(8,128)} fusion(bf16[512,2560]{1,0:T(8,128)(2,1)S(1)} %copy-done.1, bf16[256,512]{1,0:T(8,128)(2,1)S(1)} %copy-done.4, bf16[256,5120]{1,0:T(8,128)(2,1)S(1)} %bitcast.12, s32[]{:T(128)S(6)} %select_n.22), kind=kOutput, calls=%fused_computation | convolution fusion | flops 673710080 | bytes 9437188 | tf_op jit(solution)/shard_map/dot_general | solution.py:452
  (3 shorter events, 0.0 us)
Async XLA Ops:
  128.1 5.6 %copy-start = (bf16[2560,512]{1,0:T(8,128)(2,1)S(1)}, bf16[2560,512]{1,0:T(8,128)(2,1)}, u32[]{:S(2)}) copy-start(bf16[2560,512]{1,0:T(8,128)(2,1)} %get-tuple-element.13) | copy-start | bytes 7864324
  128.1 5.6 %copy-start.3 = (bf16[256,512]{1,0:T(8,128)(2,1)S(1)}, bf16[256,512]{1,0:T(8,128)(2,1)}, u32[]{:S(2)}) copy-start(bf16[256,512]{1,0:T(8,128)(2,1)} %get-tuple-element.12) | copy-start | bytes 786436
  133.7 4.7 %copy-start.1 = (bf16[512,2560]{1,0:T(8,128)(2,1)S(1)}, bf16[512,2560]{1,0:T(8,128)(2,1)}, u32[]{:S(2)}) copy-start(bf16[512,2560]{1,0:T(8,128)(2,1)} %get-tuple-element.18) | copy-start | bytes 7864324
  133.7 4.7 %copy-start.2 = (bf16[2,2,4,16,5120]{4,3,2,1,0:T(8,128)(2,1)S(1)}, bf16[2,2,4,16,5120]{4,3,2,1,0:T(8,128)(2,1)}, u32[]{:S(2)}) copy-start(bf16[2,2,4,16,5120]{4,3,2,1,0:T(8,128)(2,1)} %get-tuple-element.17) | copy-start | bytes 7864324
  133.7 4.7 %copy-start.4 = (bf16[256,512]{1,0:T(8,128)(2,1)S(1)}, bf16[256,512]{1,0:T(8,128)(2,1)}, u32[]{:S(2)}) copy-start(bf16[256,512]{1,0:T(8,128)(2,1)} %get-tuple-element.16) | copy-start | bytes 786436

commit v3 on v2

--- a/solution.py
+++ b/solution.py
@@ -13,7 +13,7 @@
 EXTRA = 128
 MESH = pl.DeviceIdType.MESH
 Y, X, Z = 0, 1, 2
-ORDERS = ((Z, X, Y), (Z, Y, X), (Z, X, Y), (Z, Y, X), (Z, X, Y))
+ORDERS = ((X, Z, Y), (Y, Z, X), (Z, X, Y), (Z, Y, X), (Z, X, Y))
 PARTS = len(ORDERS)
 bf16, f32 = jnp.bfloat16, jnp.float32
 

time: 142 us -> 143 us (level)
  no operation moved by 1% of the time
where the time goes in v3:
time: 143 us; the launch traced here: 142 us
  Pallas kernels  123 us (86%)
  matrix products  13.5 us (9%)
  other arithmetic  2.84 us (2%)
  local copies, waits for them, and re-layouts  1.78 us (1%)
    pallas_call x1, Pallas kernels, per_device(): pl.pallas_call(functools.partial(kernel, sizes, tok, width), out_shape=ou...  123 us
    dot_general x3, matrix products, own(): lax.dot_general(a, b, turned, preferred_element_type=f32) + got.astype(f32)  13.5 us

profile of v3, /device:TPU:0, one launch (start us, length us, event | category | flops | bytes accessed | tf_op | source)
XLA Modules:
  0.0 141.7 jit_solution(1781640791205548831)
XLA Ops:
  0.6 0.8 select_reduce_fusion
  1.4 0.7 convert_bitcast_fusion
  2.1 0.7 select_select_fusion
  2.8 0.8 slice.7
  3.6 0.1 reshape.34
  3.7 0.9 slice.6
  4.6 0.7 fusion.4.refs_0_
  5.3 122.8 %shard_map.121 = (bf16[2560,512]{1,0:T(8,128)(2,1)}, bf16[2560,512]{1,0:T(8,128)(2,1)}, bf16[512,2560]{1,0:T(8,128)(2,1)}, bf16[2,2,4,16,5248]{4,3,2,1,0:T(8,128...) custom-call(bf16[16,3968]{1,0:T(8,128)(2,1)} %fusion.4.refs_0_, ...), custom_call_target="tpu_custom_call" | custom-call | tf_op jit(solution)/shard_map/pallas_call | solution.py:435
  128.1 0.0 copy-start
  128.1 0.0 copy-start.3
  128.1 5.6 %convert_add_fusion.1 = f32[2560,512]{1,0:T(8,128)} fusion(bf16[2560,512]{1,0:T(8,128)(2,1)} %get-tuple-element.15, bf16[256,512]{1,0:T(8,128)(2,1)} %get-tuple-element.14, bf16[256,5248]{1,0:T(8,128)(2,1)} %bitcast.10, s32[]{:T(128)S(6)} %select_n.21), kind=kOutput, calls=%fused_computation.1 | convolution fusion | flops 673710080 | bytes 9437188 | tf_op jit(solution)/shard_map/dot_general | solution.py:452
  133.7 0.0 copy-done
  133.7 0.0 copy-done.3
  133.7 0.0 copy-start.1
  133.7 0.0 copy-start.2
  133.7 0.0 copy-start.4
  133.7 4.7 %convert_add_fusion.2 = f32[2560,512]{1,0:T(8,128)} fusion(bf16[2560,512]{1,0:T(8,128)(2,1)S(1)} %copy-done, bf16[256,512]{1,0:T(8,128)(2,1)S(1)} %copy-done.3, bf16[256,5248]{1,0:T(8,128)(2,1)} %bitcast.11, s32[]{:T(128)S(6)} %select_n.21), kind=kOutput, calls=%fused_computation.2 | convolution fusion | flops 673710080 | bytes 9437188 | tf_op jit(solution)/shard_map/dot_general | solution.py:452
  138.4 0.0 copy-done.1
  138.4 0.0 copy-done.2
  138.4 0.0 copy-done.4
  138.4 3.2 %convert_add_fusion = f32[512,2560]{1,0:T(8,128)} fusion(bf16[512,2560]{1,0:T(8,128)(2,1)S(1)} %copy-done.1, bf16[256,512]{1,0:T(8,128)(2,1)S(1)} %copy-done.4, bf16[256,5120]{1,0:T(8,128)(2,1)S(1)} %bitcast.12, s32[]{:T(128)S(6)} %select_n.22), kind=kOutput, calls=%fused_computation | convolution fusion | flops 673710080 | bytes 9437188 | tf_op jit(solution)/shard_map/dot_general | solution.py:452
  (3 shorter events, 0.0 us)
Async XLA Ops:
  128.1 5.6 %copy-start = (bf16[2560,512]{1,0:T(8,128)(2,1)S(1)}, bf16[2560,512]{1,0:T(8,128)(2,1)}, u32[]{:S(2)}) copy-start(bf16[2560,512]{1,0:T(8,128)(2,1)} %get-tuple-element.13) | copy-start | bytes 7864324
  128.1 5.6 %copy-start.3 = (bf16[256,512]{1,0:T(8,128)(2,1)S(1)}, bf16[256,512]{1,0:T(8,128)(2,1)}, u32[]{:S(2)}) copy-start(bf16[256,512]{1,0:T(8,128)(2,1)} %get-tuple-element.12) | copy-start | bytes 786436
  133.7 4.7 %copy-start.1 = (bf16[512,2560]{1,0:T(8,128)(2,1)S(1)}, bf16[512,2560]{1,0:T(8,128)(2,1)}, u32[]{:S(2)}) copy-start(bf16[512,2560]{1,0:T(8,128)(2,1)} %get-tuple-element.18) | copy-start | bytes 7864324
  133.7 4.7 %copy-start.2 = (bf16[2,2,4,16,5120]{4,3,2,1,0:T(8,128)(2,1)S(1)}, bf16[2,2,4,16,5120]{4,3,2,1,0:T(8,128)(2,1)}, u32[]{:S(2)}) copy-start(bf16[2,2,4,16,5120]{4,3,2,1,0:T(8,128)(2,1)} %get-tuple-element.17) | copy-start | bytes 7864324
  133.7 4.7 %copy-start.4 = (bf16[256,512]{1,0:T(8,128)(2,1)S(1)}, bf16[256,512]{1,0:T(8,128)(2,1)}, u32[]{:S(2)}) copy-start(bf16[256,512]{1,0:T(8,128)(2,1)} %get-tuple-element.16) | copy-start | bytes 786436
